TPU v7x, 256 devices: a whole 4x4x8 slice. The times are simulated.
256 devices in a mesh: dimer: 8 (over y_hi, x), grid: 32 (over z, y_lo, core).
Axes of the slice: x: 4, y: 4 (y_hi: 2, y_lo: 2; y = y_hi * 2 + y_lo), z: 8, core: 2. Of those that a mesh axis runs over, the one named last changes fastest.
Arguments:
- basis_values: bfloat16 [8, 40960, 1024], P('dimer', 'grid'), may hold values from -15 to 15
- aux_values: bfloat16 [8, 40960, 2048], P('dimer', 'grid'), may hold values from -6 to 6
- factors: bfloat16 [8, 512, 128], P('dimer', 'grid'), may hold values from -0.25 to 0.25
- frag_slot: int32 [8], replicated, may hold values from 0 to 7, each once
- dimer_pairs: int32 [8, 2], P('dimer'), may hold values from 0 to 7, as said below
- counts: int32 [8, 32], P('dimer', 'grid'), may hold values from 1 to 1280, 16384 in all within a row
- weights: float32 [8, 40960], P('dimer', 'grid'), may hold values from 0.000390625 to 0.0015625
- metric_inv: float32 [8, 2048, 2048], P('dimer', 'grid'), may hold values from -1 to 1, as said below
Outputs:
- frag_fock: float32 [8, 512, 512], P('dimer', 'grid')
- coupling: float32 [8, 512, 512], P('dimer', 'grid')
Inputs may be any that keep to these rules, and one draw needn't show every extreme that they name: `dimer_pairs`: each fragment is named by exactly two dimers, and the two fragments of a dimer differ. For each dimer the 32 counts sum to 16384 and the largest equals 1280. `metric_inv`: each matrix is symmetric.
All inputs are finite; a program needn't handle non-finite values. No bound on the sum of `counts` on one device may be relied on, other than what follows from the above.
Results may differ from a plain program's by a relative error of at most 0.0029.
Values may be sent and summed in bfloat16 or wider, within the bound.
A program may use at most 64 MiB of HBM per device.

v0:
```python
import jax
import jax.numpy as jnp
from jax import lax
from jax.sharding import PartitionSpec as P

exchange_coeff = 0.9847450218426964


def split_product(vector, matrix, vector_left):
    high_part = vector.astype(jnp.bfloat16)
    high_back = lax.optimization_barrier(high_part).astype(jnp.float32)
    low_part = (vector - high_back).astype(jnp.bfloat16)
    if vector_left:
        return jnp.dot(high_part, matrix, preferred_element_type=jnp.float32) + jnp.dot(
            low_part, matrix, preferred_element_type=jnp.float32
        )
    return jnp.dot(matrix, high_part, preferred_element_type=jnp.float32) + jnp.dot(
        matrix, low_part, preferred_element_type=jnp.float32
    )


def contract(left_side, right_side):
    numbers = (((0,), (0,)), ((), ()))
    return lax.dot_general(left_side, right_side, numbers, preferred_element_type=jnp.float32)


def shards(basis_values, aux_values, factors, frag_slot, dimer_pairs, counts, weights, metric_inv):
    highest = lax.Precision.HIGHEST
    basis_rows = basis_values[0]
    aux_block = aux_values[0]
    points = basis_rows.shape[0]
    frag_basis = basis_rows.shape[1] // 2
    live_count = counts[0, 0]
    position = lax.iota(jnp.int32, points)
    live_weight = jnp.where(position < live_count, weights[0], jnp.zeros((), jnp.float32))
    gathered = lax.all_gather(factors, "dimer", axis=0, tiled=True)
    frag_ids = lax.iota(jnp.int32, frag_slot.shape[0])
    wanted = jnp.sum(
        jnp.where(frag_ids[None, :] == dimer_pairs[0][:, None], frag_slot[None, :], 0), axis=1
    )
    selector = (frag_ids[None, :] == wanted[:, None]).astype(jnp.bfloat16)
    chosen = jnp.einsum(
        "as,srk->ark", selector, gathered, preferred_element_type=jnp.float32
    ).astype(jnp.bfloat16)
    dimer_factors = lax.all_gather(chosen, "grid", axis=1, tiled=True)
    orb_first = jnp.dot(
        basis_rows[:, :frag_basis], dimer_factors[0], preferred_element_type=jnp.float32
    )
    orb_second = jnp.dot(
        basis_rows[:, frag_basis:], dimer_factors[1], preferred_element_type=jnp.float32
    )
    density = (
        jnp.sum(orb_first * orb_first, axis=1) + jnp.sum(orb_second * orb_second, axis=1)
    ) / (2.0 * dimer_factors.shape[2])
    exchange = -exchange_coeff * jnp.cbrt(density)
    weighted_density = live_weight * density
    fitted = lax.psum(split_product(weighted_density, aux_block, True), "grid")
    coef_rows = jnp.dot(metric_inv[0], fitted, precision=highest)
    coefficients = lax.all_gather(coef_rows, "grid", axis=0, tiled=True)
    coulomb = split_product(coefficients, aux_block, False)
    potential_total, weight_sum = lax.psum(
        (jnp.sum(live_weight * (coulomb + exchange)), jnp.sum(live_weight)), "grid"
    )
    average = potential_total / weight_sum
    potential = live_weight * (coulomb + exchange - average)
    weighted_basis = (basis_rows * potential[:, None]).astype(jnp.bfloat16)
    half_rows = frag_basis // lax.axis_size("grid")
    groups = 2 * half_rows * lax.axis_size("grid") // (2 * half_rows)
    first_index = jnp.int32(0) // 2
    left_first = lax.dynamic_slice_in_dim(
        weighted_basis, first_index, groups * half_rows, 1
    ).reshape(points, groups, half_rows)
    left_second = lax.dynamic_slice_in_dim(
        weighted_basis, frag_basis, groups * half_rows, 1
    ).reshape(points, groups, half_rows)
    left_side = jnp.concatenate([left_first, left_second], axis=2).reshape(
        points, 2 * half_rows * lax.axis_size("grid")
    )
    shares = lax.psum_scatter(
        contract(left_side, basis_rows), "grid", scatter_dimension=0, tiled=True
    )
    own_first = shares[:half_rows, :frag_basis]
    own_cross = shares[:half_rows, frag_basis:]
    own_second = shares[half_rows:, frag_basis:]
    is_first = (frag_ids == dimer_pairs[0, 0])[:, None, None]
    is_second = (frag_ids == dimer_pairs[0, 1])[:, None, None]
    fock_terms = jnp.where(is_first, own_first[None], jnp.zeros((), jnp.float32)) + jnp.where(
        is_second, own_second[None], jnp.zeros((), jnp.float32)
    )
    frag_fock = lax.psum_scatter(fock_terms, "dimer", scatter_dimension=0, tiled=True)
    return (frag_fock, own_cross[None])


def solution(mesh):
    placed = (
        P("dimer", "grid", None),
        P("dimer", "grid", None),
        P("dimer", "grid", None),
        P(),
        P("dimer", None),
        P("dimer", "grid"),
        P("dimer", "grid"),
        P("dimer", "grid", None),
    )
    return jax.shard_map(
        shards,
        mesh=mesh,
        in_specs=placed,
        out_specs=(P("dimer", "grid", None), P("dimer", "grid", None)),
        check_vma=False,
    )
```

profile of v0, /device:TPU:2, one launch (start us, length us, event | category | flops | bytes accessed | tf_op | source)
XLA Modules:
  0.0 475.2 jit_solution(4176700981948331173)
XLA Ops:
  8.0 3.0 copy.17
  11.0 34.4 %all_gather.9 = bf16[8,16,128]{2,1,0:T(8,128)(2,1)S(1)} all-gather(bf16[1,16,128]{2,1,0:T(8,128)(2,1)S(1)} %copy-done.4), channel_id=1, replica_groups=mesh['dimer'=8,'grid'=32] {'dimer'}, dimensions={0}, use_global_device_ids=true | all-gather | bytes 36864 | tf_op jit(solution)/shard_map/all_gather | solution.py:36
  45.7 37.0 %all_gather.10 = bf16[2,512,128]{2,0,1:T(2,128)(2,1)S(1)} all-gather(bf16[2,16,128]{2,0,1:T(2,128)(2,1)S(1)} %convolution_convert_fusion), channel_id=1, replica_groups=mesh['dimer'=8,'grid'=32] {'grid'}, dimensions={1}, use_global_device_ids=true | all-gather | bytes 270336 | tf_op jit(solution)/shard_map/all_gather | solution.py:45
  83.5 0.4 fusion.15
  84.0 3.4 fusion.4
  87.4 0.6 copy-done.1
  88.0 0.8 fusion.6
  88.8 54.3 %psum.21 = f32[2048]{0:T(1024)S(1)} all-reduce(f32[2048]{0:T(1024)S(1)} %add.37), channel_id=1, replica_groups=mesh['dimer'=8,'grid'=32] {'grid'}, use_global_device_ids=true, to_apply=%region_3.4 | all-reduce | flops 2048 | bytes 16384 | tf_op jit(solution)/shard_map/psum | solution.py:57
  143.1 0.5 convolution_bitcast_fusion
  143.7 0.6 dynamic-slice
  145.2 54.0 %all-reduce = f32[2048]{0:T(1024)S(1)} all-reduce(f32[2048]{0:T(1024)S(1)} %dynamic-update-slice), channel_id=1, replica_groups=mesh['dimer'=8,'grid'=32] {'grid'}, use_global_device_ids=true, to_apply=%add | all-reduce | flops 2048 | bytes 16384
  199.2 4.0 fusion.21
  203.2 4.0 fusion.18
  207.2 0.7 fusion.27
  207.9 53.6 %all-reduce.1 = (f32[]{:T(128)}, f32[]{:T(128)}) all-reduce(f32[]{:T(128)} %get-tuple-element.3, f32[]{:T(128)} %get-tuple-element.2), channel_id=1, replica_groups=mesh['dimer'=8,'grid'=32] {'grid'}, use_global_device_ids=true, to_apply=%region_5.6 | all-reduce | flops 2 | bytes 16 | tf_op jit(solution)/shard_map/psum | solution.py:61
  262.8 0.5 multiply_convert_fusion
  263.8 1.4 copy-done.2
  265.2 4.4 fusion.8
  269.7 0.6 fusion.45
  270.3 1.3 iota_compare_fusion.1
  271.6 119.2 %reduce-scatter.3.cloned.1.call-done = f32[32,1024]{1,0:T(8,128)} async-done(((f32[1024,1024]{1,0:T(8,128)}), f32[32,1024]{1,0:T(8,128)}) %reduce-scatter.3.cloned.1.call-update) | async-done | bytes 131088 | tf_op jit(solution)/shard_map/reduce_scatter | solution.py:79
  390.7 1.4 slice_bitcast_fusion
  392.1 0.8 select_add_fusion
  393.0 75.4 %reduce-scatter.5.cloned.1.call-done = f32[1,16,512]{2,1,0:T(8,128)} async-done(((f32[8,16,512]{2,1,0:T(8,128)}), f32[1,16,512]{2,1,0:T(8,128)}) %reduce-scatter.5.cloned.1.call-update) | async-done | bytes 32784 | tf_op jit(solution)/shard_map/reduce_scatter | solution.py:90
  (36 shorter events, 2.2 us)
Async XLA Ops:
  7.2 136.0 %copy-start = (f32[1,64,2048]{2,1,0:T(8,128)S(1)}, f32[1,64,2048]{2,1,0:T(8,128)}, u32[]{:S(2)}) copy-start(f32[1,64,2048]{2,1,0:T(8,128)} %param.15) | copy-start | bytes 1572868
  7.2 383.6 %reduce-scatter.3.cloned.1.call-start = ((), (), s32[]{:S(2)}) async-start(), calls=%async_computation.2 | async-start | bytes 4325376 | tf_op jit(solution)/shard_map/reduce_scatter | solution.py:79
  7.9 3.0 copy-start.4
  7.9 37.4 %copy-start.5 = (s32[1,2]{1,0:T(1,128)S(1)}, s32[1,2]{1,0:T(1,128)}, u32[]{:S(2)}) copy-start(s32[1,2]{1,0:T(1,128)} %param.12) | copy-start | bytes 28
  7.9 37.4 %copy-start.6 = (s32[8]{0:T(128)S(1)}, s32[8]{0:T(128)}, u32[]{:S(2)}) copy-start(s32[8]{0:T(128)} %param.11) | copy-start | bytes 100
  11.0 72.9 %copy-start.3 = (f32[1,1280]{1,0:T(1,128)S(1)}, f32[1,1280]{1,0:T(1,128)}, u32[]{:S(2)}) copy-start(f32[1,1280]{1,0:T(1,128)} %param.14) | copy-start | bytes 15364
  83.9 4.0 copy-start.1
  88.0 55.7 %copy-start.7 = (u32[256]{0:T(256)S(1)}, u32[256]{0:T(256)}, u32[]{:S(2)}) copy-start(u32[256]{0:T(256)} %constant.35) | copy-start | bytes 3076
  263.5 1.7 copy-start.2
  269.6 198.7 %reduce-scatter.5.cloned.1.call-start = ((), (), s32[]{:S(2)}) async-start(), calls=%async_computation.3 | async-start | bytes 294912 | tf_op jit(solution)/shard_map/reduce_scatter | solution.py:90
Sparse Core Ops, SparseCore 0:
  269.7 120.9 reduce-scatter.2
  395.2 73.1 reduce-scatter.4
where the time goes:
time: 476 us; the launch traced here: 475 us
  blocking collectives  233 us (49%)
  waiting for transfers between devices  195 us (41%)
  matrix products  18 us (4%)
  between operations  16.9 us (4%)
  local copies, waits for them, and re-layouts  8.46 us (2%)
    reduce_scatter x1, waiting for transfers between devices, shards(): lax.psum_scatter(contract(left_side, basis_rows), 'grid', scatter_dimensi...  119 us
    reduce_scatter x1, waiting for transfers between devices, shards(): lax.psum_scatter(fock_terms, 'dimer', scatter_dimension=0, tiled=True)  75.4 us
    psum x1, blocking collectives, shards(): fitted = lax.psum(split_product(weighted_density, aux_block, True), 'grid')  54.3 us
    unnamed x1, blocking collectives  54 us
    psum x1, blocking collectives, shards(): lax.psum((jnp.sum(live_weight * (coulomb + exchange)), jnp.sum(live_weigh...  53.6 us
    all_gather x1, blocking collectives, shards(): dimer_factors = lax.all_gather(chosen, 'grid', axis=1, tiled=True)  37 us
    all_gather x1, blocking collectives, shards(): gathered = lax.all_gather(factors, 'dimer', axis=0, tiled=True)  34.4 us
  transfers between devices with their start and end apart: 2, of which 2 were waited for; matrix products, arithmetic and copies ran while one was open for 0% of the time, Pallas kernels for 0%

commit v1 on v0

--- a/solution.py
+++ b/solution.py
@@ -54,7 +54,9 @@
     ) / (2.0 * dimer_factors.shape[2])
     exchange = -exchange_coeff * jnp.cbrt(density)
     weighted_density = live_weight * density
-    fitted = lax.psum(split_product(weighted_density, aux_block, True), "grid")
+    fitted = jnp.sum(
+        lax.all_gather(split_product(weighted_density, aux_block, True), "grid"), axis=0
+    )
     coef_rows = jnp.dot(metric_inv[0], fitted, precision=highest)
     coefficients = lax.all_gather(coef_rows, "grid", axis=0, tiled=True)
     coulomb = split_product(coefficients, aux_block, False)

time: 476 us -> 456 us (0.958)
  blocking collectives: 233 us -> 212 us
    psum x1 -> x0, blocking collectives: 54.3 us -> none  [shards(): fitted = lax.psum(split_product(weighted_density, aux_block, True), 'grid')]
    all_gather x0 -> x1, blocking collectives: none -> 31.4 us  [shards(): lax.all_gather(split_product(weighted_density, aux_block, True), 'grid')]
where the time goes in v1:
time: 456 us; the launch traced here: 455 us
  blocking collectives  212 us (46%)
  waiting for transfers between devices  194 us (43%)
  matrix products  18 us (4%)
  between operations  16.9 us (4%)
  local copies, waits for them, and re-layouts  9.2 us (2%)
  other arithmetic  4.85 us (1%)
    reduce_scatter x1, waiting for transfers between devices, shards(): lax.psum_scatter(contract(left_side, basis_rows), 'grid', scatter_dimensi...  119 us
    reduce_scatter x1, waiting for transfers between devices, shards(): lax.psum_scatter(fock_terms, 'dimer', scatter_dimension=0, tiled=True)  75.2 us
    unnamed x1, blocking collectives  55.6 us
    psum x1, blocking collectives, shards(): lax.psum((jnp.sum(live_weight * (coulomb + exchange)), jnp.sum(live_weigh...  53.6 us
    all_gather x1, blocking collectives, shards(): dimer_factors = lax.all_gather(chosen, 'grid', axis=1, tiled=True)  37 us
    all_gather x1, blocking collectives, shards(): gathered = lax.all_gather(factors, 'dimer', axis=0, tiled=True)  34.4 us
    all_gather x1, blocking collectives, shards(): lax.all_gather(split_product(weighted_density, aux_block, True), 'grid')  31.4 us
  transfers between devices with their start and end apart: 2, of which 2 were waited for; matrix products, arithmetic and copies ran while one was open for 0% of the time, Pallas kernels for 0%

profile of v1, /device:TPU:2, one launch (start us, length us, event | category | flops | bytes accessed | tf_op | source)
XLA Modules:
  0.0 455.1 jit_solution(7436727656651107146)
XLA Ops:
  8.0 3.0 copy.17
  11.0 34.4 %all_gather.15 = bf16[8,16,128]{2,1,0:T(8,128)(2,1)S(1)} all-gather(bf16[1,16,128]{2,1,0:T(8,128)(2,1)S(1)} %copy-done.4), channel_id=1, replica_groups=mesh['dimer'=8,'grid'=32] {'dimer'}, dimensions={0}, use_global_device_ids=true | all-gather | bytes 36864 | tf_op jit(solution)/shard_map/all_gather | solution.py:36
  45.7 37.0 %all_gather.16 = bf16[2,512,128]{2,0,1:T(2,128)(2,1)S(1)} all-gather(bf16[2,16,128]{2,0,1:T(2,128)(2,1)S(1)} %convolution_convert_fusion), channel_id=1, replica_groups=mesh['dimer'=8,'grid'=32] {'grid'}, dimensions={1}, use_global_device_ids=true | all-gather | bytes 270336 | tf_op jit(solution)/shard_map/all_gather | solution.py:45
  84.0 3.4 fusion.4
  87.4 0.6 copy-done.1
  88.0 0.8 fusion.6
  88.8 31.4 %all-gather = f32[65536]{0:T(1024)S(1)} all-gather(f32[2048]{0:T(1024)S(1)} %add.35), channel_id=2, replica_groups=mesh['dimer'=8,'grid'=32] {'grid'}, dimensions={0}, use_global_device_ids=true | all-gather | bytes 270336 | tf_op jit(solution)/shard_map/all_gather | solution.py:58
  120.2 0.7 reshape.55
  120.9 1.0 reduce_sum.57
  121.9 0.5 convolution_bitcast_fusion
  122.4 0.6 dynamic-slice
  124.0 55.6 %all-reduce = f32[2048]{0:T(1024)S(1)} all-reduce(f32[2048]{0:T(1024)S(1)} %dynamic-update-slice), channel_id=1, replica_groups=mesh['dimer'=8,'grid'=32] {'grid'}, use_global_device_ids=true, to_apply=%add | all-reduce | flops 2048 | bytes 16384
  179.6 4.0 fusion.21
  183.6 4.0 fusion.18
  187.5 0.7 fusion.27
  188.2 53.6 %all-reduce.1 = (f32[]{:T(128)}, f32[]{:T(128)}) all-reduce(f32[]{:T(128)} %get-tuple-element.3, f32[]{:T(128)} %get-tuple-element.2), channel_id=1, replica_groups=mesh['dimer'=8,'grid'=32] {'grid'}, use_global_device_ids=true, to_apply=%region_5.6 | all-reduce | flops 2 | bytes 16 | tf_op jit(solution)/shard_map/psum | solution.py:63
  244.2 1.4 copy-done.2
  245.5 4.4 fusion.8
  250.0 0.6 fusion.45
  250.6 1.3 iota_compare_fusion.1
  251.9 118.9 %reduce-scatter.3.cloned.1.call-done = f32[32,1024]{1,0:T(8,128)} async-done(((f32[1024,1024]{1,0:T(8,128)}), f32[32,1024]{1,0:T(8,128)}) %reduce-scatter.3.cloned.1.call-update) | async-done | bytes 131088 | tf_op jit(solution)/shard_map/reduce_scatter | solution.py:81
  370.9 1.4 slice_bitcast_fusion
  372.3 0.8 select_add_fusion
  373.1 75.2 %reduce-scatter.5.cloned.1.call-done = f32[1,16,512]{2,1,0:T(8,128)} async-done(((f32[8,16,512]{2,1,0:T(8,128)}), f32[1,16,512]{2,1,0:T(8,128)}) %reduce-scatter.5.cloned.1.call-update) | async-done | bytes 32784 | tf_op jit(solution)/shard_map/reduce_scatter | solution.py:92
  (38 shorter events, 3.0 us)
Async XLA Ops:
  7.2 114.7 %copy-start = (f32[1,64,2048]{2,1,0:T(8,128)S(1)}, f32[1,64,2048]{2,1,0:T(8,128)}, u32[]{:S(2)}) copy-start(f32[1,64,2048]{2,1,0:T(8,128)} %param.15) | copy-start | bytes 1572868
  7.2 363.7 %reduce-scatter.3.cloned.1.call-start = ((), (), s32[]{:S(2)}) async-start(), calls=%async_computation.2 | async-start | bytes 4325376 | tf_op jit(solution)/shard_map/reduce_scatter | solution.py:81
  7.9 3.0 copy-start.4
  7.9 37.4 %copy-start.5 = (s32[1,2]{1,0:T(1,128)S(1)}, s32[1,2]{1,0:T(1,128)}, u32[]{:S(2)}) copy-start(s32[1,2]{1,0:T(1,128)} %param.12) | copy-start | bytes 28
  7.9 37.4 %copy-start.6 = (s32[8]{0:T(128)S(1)}, s32[8]{0:T(128)}, u32[]{:S(2)}) copy-start(s32[8]{0:T(128)} %param.11) | copy-start | bytes 100
  11.0 72.9 %copy-start.3 = (f32[1,1280]{1,0:T(1,128)S(1)}, f32[1,1280]{1,0:T(1,128)}, u32[]{:S(2)}) copy-start(f32[1,1280]{1,0:T(1,128)} %param.14) | copy-start | bytes 15364
  83.9 4.0 copy-start.1
  88.0 34.4 %copy-start.7 = (u32[256]{0:T(256)S(1)}, u32[256]{0:T(256)}, u32[]{:S(2)}) copy-start(u32[256]{0:T(256)} %constant.35) | copy-start | bytes 3076
  243.8 1.7 copy-start.2
  250.0 198.3 %reduce-scatter.5.cloned.1.call-start = ((), (), s32[]{:S(2)}) async-start(), calls=%async_computation.3 | async-start | bytes 294912 | tf_op jit(solution)/shard_map/reduce_scatter | solution.py:92
Sparse Core Ops, SparseCore 0:
  250.1 120.7 reduce-scatter.2
  375.3 72.9 reduce-scatter.4

commit v2 on v0

--- a/solution.py
+++ b/solution.py
@@ -42,7 +42,9 @@
     chosen = jnp.einsum(
         "as,srk->ark", selector, gathered, preferred_element_type=jnp.float32
     ).astype(jnp.bfloat16)
-    dimer_factors = lax.all_gather(chosen, "grid", axis=1, tiled=True)
+    dimer_factors = jnp.concatenate(
+        lax.all_to_all(jnp.stack([chosen] * lax.axis_size("grid")), "grid", 0, 0), axis=1
+    )
     orb_first = jnp.dot(
         basis_rows[:, :frag_basis], dimer_factors[0], preferred_element_type=jnp.float32
     )

time: 476 us -> 460 us (0.966)
  blocking collectives: 233 us -> 197 us
  starting transfers between devices: 0.08 us -> 9.05 us
  waiting for transfers between devices: 195 us -> 201 us
    all_gather x1 -> x0, blocking collectives: 37 us -> none  [shards(): dimer_factors = lax.all_gather(chosen, 'grid', axis=1, tiled=True)]
    all_to_all x0 -> x1, starting transfers between devices: none -> 8.97 us  [shards(): lax.all_to_all(jnp.stack([chosen] * lax.axis_size('grid')), 'grid', 0, 0)]
    all_to_all x0 -> x1, waiting for transfers between devices: none -> 5.71 us  [shards(): lax.all_to_all(jnp.stack([chosen] * lax.axis_size('grid')), 'grid', 0, 0)]
  transfers between devices with their start and end apart: 2 -> 3, of which waited for: 2 -> 3; matrix products, arithmetic and copies ran while one was open for 0% -> 2% of each run, Pallas kernels for 0% -> 0%
where the time goes in v2:
time: 460 us; the launch traced here: 459 us
  waiting for transfers between devices  201 us (44%)
  blocking collectives  197 us (43%)
  matrix products  20.8 us (5%)
  between operations  16.9 us (4%)
  local copies, waits for them, and re-layouts  10.2 us (2%)
  starting transfers between devices  9.05 us (2%)
    reduce_scatter x1, waiting for transfers between devices, shards(): lax.psum_scatter(contract(left_side, basis_rows), 'grid', scatter_dimensi...  120 us
    reduce_scatter x1, waiting for transfers between devices, shards(): lax.psum_scatter(fock_terms, 'dimer', scatter_dimension=0, tiled=True)  75.1 us
    psum x1, blocking collectives, shards(): fitted = lax.psum(split_product(weighted_density, aux_block, True), 'grid')  54.3 us
    unnamed x1, blocking collectives  54 us
    psum x1, blocking collectives, shards(): lax.psum((jnp.sum(live_weight * (coulomb + exchange)), jnp.sum(live_weigh...  53.7 us
    all_gather x1, blocking collectives, shards(): gathered = lax.all_gather(factors, 'dimer', axis=0, tiled=True)  34.6 us
  transfers between devices with their start and end apart: 3, of which 3 were waited for; matrix products, arithmetic and copies ran while one was open for 2% of the time, Pallas kernels for 0%

profile of v2, /device:TPU:2, one launch (start us, length us, event | category | flops | bytes accessed | tf_op | source)
XLA Modules:
  0.0 459.3 jit_solution(3493336685778789119)
XLA Ops:
  7.2 34.6 %all_gather.6 = bf16[8,16,128]{2,1,0:T(8,128)(2,1)S(1)} all-gather(bf16[1,16,128]{2,1,0:T(8,128)(2,1)} %param.10), channel_id=1, replica_groups=mesh['dimer'=8,'grid'=32] {'dimer'}, dimensions={0}, use_global_device_ids=true | all-gather | bytes 36864 | tf_op jit(solution)/shard_map/all_gather | solution.py:36
  41.8 0.9 fusion.39
  42.9 0.7 stack.2
  43.6 9.0 %all-to-all-start = ((bf16[32,2,16,128]{3,2,1,0:T(8,128)(2,1)}), bf16[32,2,16,128]{3,2,1,0:T(8,128)(2,1)S(1)}, u32[]{:S(2)}, u32[]{:S(2)}) async-start(bf16[32,2,16,128]{3,2,1,0:T(8,128)(2,1)} %stack.2), calls=%async_computation | async-start | bytes 524288 | tf_op jit(solution)/shard_map/all_to_all | solution.py:46
  53.3 4.5 copy.18
  57.8 0.6 dynamic-slice
  59.1 5.7 %all-to-all-done = bf16[32,2,16,128]{3,2,1,0:T(8,128)(2,1)S(1)} async-done(((bf16[32,2,16,128]{3,2,1,0:T(8,128)(2,1)}), bf16[32,2,16,128]{3,2,1,0:T(8,128)(2,1)S(1)}, u32[]{:S(2)}, u32[]{:S(2)}) %all-to-all-start) | async-done | bytes 262176 | tf_op jit(solution)/shard_map/all_to_all | solution.py:46
  64.8 1.8 fusion.12
  66.7 1.7 fusion.15
  68.4 3.3 fusion.4
  71.7 0.8 fusion.6
  72.5 54.3 %psum.21 = f32[2048]{0:T(1024)S(1)} all-reduce(f32[2048]{0:T(1024)S(1)} %add.37), channel_id=1, replica_groups=mesh['dimer'=8,'grid'=32] {'grid'}, use_global_device_ids=true, to_apply=%region_3.4 | all-reduce | flops 2048 | bytes 16384 | tf_op jit(solution)/shard_map/psum | solution.py:59
  127.6 54.0 %all-reduce = f32[2048]{0:T(1024)S(1)} all-reduce(f32[2048]{0:T(1024)S(1)} %dynamic-update-slice), channel_id=1, replica_groups=mesh['dimer'=8,'grid'=32] {'grid'}, use_global_device_ids=true, to_apply=%add | all-reduce | flops 2048 | bytes 16384
  181.6 4.0 fusion.21
  185.6 4.1 fusion.18
  189.7 0.6 fusion.27
  190.3 53.7 %all-reduce.1 = (f32[]{:T(128)}, f32[]{:T(128)}) all-reduce(f32[]{:T(128)} %get-tuple-element.3, f32[]{:T(128)} %get-tuple-element.2), channel_id=1, replica_groups=mesh['dimer'=8,'grid'=32] {'grid'}, use_global_device_ids=true, to_apply=%region_5.6 | all-reduce | flops 2 | bytes 16 | tf_op jit(solution)/shard_map/psum | solution.py:63
  246.4 1.4 copy-done.2
  247.8 4.4 fusion.8
  253.4 1.3 iota_compare_fusion.1
  254.7 120.4 %reduce-scatter.3.cloned.1.call-done = f32[32,1024]{1,0:T(8,128)} async-done(((f32[1024,1024]{1,0:T(8,128)}), f32[32,1024]{1,0:T(8,128)}) %reduce-scatter.3.cloned.1.call-update) | async-done | bytes 131088 | tf_op jit(solution)/shard_map/reduce_scatter | solution.py:81
  375.1 1.4 slice_bitcast_fusion
  376.5 0.8 select_add_fusion
  377.3 75.1 %reduce-scatter.5.cloned.1.call-done = f32[1,16,512]{2,1,0:T(8,128)} async-done(((f32[8,16,512]{2,1,0:T(8,128)}), f32[1,16,512]{2,1,0:T(8,128)}) %reduce-scatter.5.cloned.1.call-update) | async-done | bytes 32784 | tf_op jit(solution)/shard_map/reduce_scatter | solution.py:92
  (40 shorter events, 3.4 us)
Async XLA Ops:
  7.2 119.7 %copy-start = (f32[1,64,2048]{2,1,0:T(8,128)S(1)}, f32[1,64,2048]{2,1,0:T(8,128)}, u32[]{:S(2)}) copy-start(f32[1,64,2048]{2,1,0:T(8,128)} %param.15) | copy-start | bytes 1572868
  43.6 21.2 %all-to-all-start = ((bf16[32,2,16,128]{3,2,1,0:T(8,128)(2,1)}), bf16[32,2,16,128]{3,2,1,0:T(8,128)(2,1)S(1)}, u32[]{:S(2)}, u32[]{:S(2)}) async-start(bf16[32,2,16,128]{3,2,1,0:T(8,128)(2,1)} %stack.2), calls=%async_computation | async-start | bytes 524288 | tf_op jit(solution)/shard_map/all_to_all | solution.py:46
  52.6 322.5 %reduce-scatter.3.cloned.1.call-start = ((), (), s32[]{:S(2)}) async-start(), calls=%async_computation.3 | async-start | bytes 4325376 | tf_op jit(solution)/shard_map/reduce_scatter | solution.py:81
  53.3 4.5 copy-start.3
  53.3 4.5 copy-start.5
  53.3 18.4 %slice-start = ((s8[5242880]{0:T(1024)(128)(4,1)}), s8[1048576]{0:T(1024)(128)(4,1)S(1)}, s32[]{:S(2)}) async-start(s8[5242880]{0:T(1024)(128)(4,1)} %bitcast.57), calls=%async_computation.5 | async-start | bytes 2097152
  64.8 6.9 %slice-start.1 = ((s8[5242880]{0:T(1024)(128)(4,1)}), s8[4194304]{0:T(1024)(128)(4,1)S(1)}, s32[]{:S(2)}) async-start(s8[5242880]{0:T(1024)(128)(4,1)} %bitcast.57), calls=%async_computation.6 | async-start | bytes 8388608
  185.6 59.8 %copy-start.1 = (bf16[1,1280,1024]{1,2,0:T(8,128)(2,1)S(1)}, bf16[1,1280,1024]{1,2,0:T(8,128)(2,1)}, u32[]{:S(2)}) copy-start(bf16[1,1280,1024]{1,2,0:T(8,128)(2,1)} %copy.18) | copy-start | bytes 7864324
  246.0 1.7 copy-start.2
  252.2 0.7 copy-start.4
  252.2 200.3 %reduce-scatter.5.cloned.1.call-start = ((), (), s32[]{:S(2)}) async-start(), calls=%async_computation.4 | async-start | bytes 294912 | tf_op jit(solution)/shard_map/reduce_scatter | solution.py:92
Sparse Core Ops, SparseCore 0:
  252.3 122.7 reduce-scatter.2
  379.5 72.8 reduce-scatter.4
